TPU v7x, 32 devices: a whole 2x2x4 slice. The times are simulated.
32 devices in a mesh: grp: 2 (over y), ffn: 4 (over z), wid: 2 (over x), sub: 2 (over core).
Axes of the slice: x: 2, y: 2, z: 4, core: 2. Of those that a mesh axis runs over, the one named last changes fastest.
Arguments:
- states: bfloat16 [2048, 16384], P(('grp', 'ffn'), ('wid', 'sub')), parts along dimension 0
- norm_gain: bfloat16 [16384], P(('wid', 'sub')), may hold values from 0.099609375 to 1.8984375
- query_weight: bfloat16 [16384, 16384], P(('wid', 'sub'), 'ffn')
- key_weight: bfloat16 [16384, 1024], P(('wid', 'sub'), 'ffn')
- value_weight: bfloat16 [16384, 1024], P(('wid', 'sub'), 'ffn'), may hold values from -0.046875 to 0.046875
- output_weight: bfloat16 [16384, 16384], P('ffn', ('wid', 'sub')), may hold values from -0.125 to 0.125
- segments: int32 [2048], P('grp'), parts along dimension 0, may hold values from 0 to 3, never falling along the last dimension, each value on 1 to 512 neighbouring positions
Outputs:
- attention_out: bfloat16 [2048, 16384], P(('grp', 'ffn'), ('wid', 'sub')), parts along dimension 0
There are 2 independent parts, one for each index of `grp`. A program takes and returns all parts, laid end to end along the dimension named above; an argument that names none is the same for every part. Nothing has to cross between parts.
Inputs may be any that keep to these rules, and one draw needn't show every extreme that they name: `segments`: document numbers never fall along the prompt; each of the 4 documents has 1 to 512 tokens, one exactly 512.
All inputs are finite; a program needn't handle non-finite values.
Results may differ from a plain program's by a relative error of at most 0.034.
Values may be sent and summed in bfloat16 or wider, within the bound.
A program may use at most 256 MiB of HBM per device.

v0:
```python
import jax
import jax.numpy as jnp
from jax import lax
from jax.sharding import PartitionSpec as P

KVH = 8
HD = 128


EPS = 1e-05
THETA = 500000.0
NEGATIVE = -1e30


def swapped(value, axis, distance):
    mask = 2**distance
    pairs = [(source, source ^ mask) for source in range(lax.axis_size(axis))]
    return lax.ppermute(value, axis, pairs)


def rope_tables(positions):
    half = HD // 2
    freqs = THETA ** (-(jnp.arange(half, dtype=jnp.float32) * 2.0 / HD))
    angles = positions.astype(jnp.float32)[:, None] * freqs[None, :]
    return (jnp.cos(angles), jnp.sin(angles))


def rotate(tensor, cosine, sine):
    half = HD // 2
    first = tensor[..., :half]
    second = tensor[..., half:]
    cosine = cosine[:, None, :]
    sine = sine[:, None, :]
    return jnp.concatenate(
        [first * cosine - second * sine, second * cosine + first * sine], axis=-1
    )


def body(states, norm_gain, query_weight, key_weight, value_weight, output_weight, segments):
    wide_states = states.astype(jnp.float32)
    width = states.shape[1] * lax.axis_size(("wid", "sub"))
    square_sum = lax.psum(jnp.sum(wide_states * wide_states, axis=1), ("wid", "sub"))
    scaling = lax.rsqrt(square_sum[:, None] / width + EPS)
    normed = (wide_states * scaling * norm_gain.astype(jnp.float32)[None, :]).astype(jnp.bfloat16)
    query_cols = query_weight.shape[1]
    key_cols = key_weight.shape[1]
    piece = lax.all_gather(normed, "ffn", axis=0, tiled=True)
    partial_value = jnp.concatenate(
        [
            jnp.dot(piece, query_weight, preferred_element_type=jnp.float32),
            jnp.dot(piece, key_weight, preferred_element_type=jnp.float32),
            jnp.dot(piece, value_weight, preferred_element_type=jnp.float32),
        ],
        axis=1,
    )
    total_rows = partial_value.shape[0]
    query_part = partial_value[:, :query_cols]
    key_part = partial_value[:, query_cols : query_cols + key_cols]
    value_part = partial_value[:, query_cols + key_cols :]
    block_rows = total_rows // lax.axis_size(("wid", "sub"))
    query_sum = lax.psum_scatter(
        query_part.astype(jnp.bfloat16), ("wid", "sub"), scatter_dimension=0, tiled=True
    ).astype(jnp.float32)
    key_sum, value_sum = (
        lax.psum(key_part.astype(jnp.bfloat16), ("wid", "sub")).astype(jnp.float32),
        lax.psum(value_part.astype(jnp.bfloat16), ("wid", "sub")).astype(jnp.float32),
    )
    first_row = lax.axis_index(("wid", "sub")) * block_rows
    kv_stack = jnp.stack([key_sum, value_sum])
    reach = max(1, lax.axis_size("ffn") // KVH)
    position = lax.axis_index("ffn")
    for bit_number in range(reach.bit_length() - 1):
        partner = swapped(kv_stack.astype(jnp.bfloat16), "ffn", bit_number).astype(kv_stack.dtype)
        lower = position // 2**bit_number % 2 == 0
        kv_stack = jnp.where(
            lower,
            jnp.concatenate([kv_stack, partner], axis=2),
            jnp.concatenate([partner, kv_stack], axis=2),
        )
    kv_heads = kv_stack.shape[2] // HD
    all_rows = jnp.arange(total_rows, dtype=jnp.int32)
    cosine, sine = rope_tables(all_rows)
    keys = rotate(kv_stack[0].reshape(total_rows, kv_heads, HD), cosine, sine).astype(jnp.bfloat16)
    values = kv_stack[1].reshape(total_rows, kv_heads, HD).astype(jnp.bfloat16)
    heads_here = query_cols // HD
    per_group = heads_here // kv_heads
    query_count = query_sum.shape[0]
    row_ids = first_row + jnp.arange(query_count, dtype=jnp.int32)
    query_cos, query_sin = rope_tables(row_ids)
    queries = (
        rotate(query_sum.reshape(query_count, heads_here, HD), query_cos, query_sin) * HD ** (-0.5)
    ).astype(jnp.bfloat16)
    queries = queries.reshape(query_count, kv_heads, per_group, HD)
    query_segments = lax.dynamic_slice_in_dim(segments, first_row, query_count)

    def attend(block_index):
        allowed = (query_segments[:, None] == segments[None, :]) & (
            all_rows[None, :] <= row_ids[:, None]
        )
        scores = jnp.einsum("tcpd,scd->cpts", queries, keys, preferred_element_type=jnp.float32)
        masked = jnp.where(allowed[None, None], scores, NEGATIVE)
        highest = jnp.max(masked, axis=-1, keepdims=True)
        weights = jnp.exp(masked - highest)
        total = jnp.sum(weights, axis=-1, keepdims=True)
        probs = (weights / total).astype(jnp.bfloat16)
        result = jnp.einsum("cpts,scd->tcpd", probs, values, preferred_element_type=jnp.float32)
        return result.astype(jnp.bfloat16).reshape(block_rows, heads_here * HD)

    attended = lax.map(attend, jnp.arange(query_count // block_rows, dtype=jnp.int32))
    attended = attended.reshape(query_count, heads_here * HD)
    terms = jnp.dot(
        lax.all_gather(attended, ("wid", "sub"), axis=0, tiled=True),
        output_weight,
        preferred_element_type=jnp.float32,
    )
    mixed = lax.psum_scatter(terms.astype(jnp.bfloat16), "ffn", scatter_dimension=0, tiled=True)
    return mixed


def solution(mesh):
    in_specs = (
        P(("grp", "ffn"), ("wid", "sub")),
        P(("wid", "sub")),
        P(("wid", "sub"), "ffn"),
        P(("wid", "sub"), "ffn"),
        P(("wid", "sub"), "ffn"),
        P("ffn", ("wid", "sub")),
        P("grp"),
    )
    out_specs = P(("grp", "ffn"), ("wid", "sub"))
    return jax.shard_map(body, mesh=mesh, in_specs=in_specs, out_specs=out_specs, check_vma=False)
```

profile of v0, /device:TPU:0, one launch (start us, length us, event | category | flops | bytes accessed | tf_op | source)
XLA Modules:
  0.0 597.9 jit_solution(16878747305718503453)
XLA Ops:
  6.5 2.2 fusion.7
  8.8 8.3 %psum.21 = f32[256]{0:T(256)S(1)} all-reduce(f32[256]{0:T(256)S(1)} %fusion.7), channel_id=1, replica_groups=mesh['grp'=2,'ffn'=4,'wid'=2,'sub'=2] {'wid','sub'}, use_global_device_ids=true, to_apply=%region_1.0 | all-reduce | flops 256 | bytes 2048 | tf_op jit(solution)/shard_map/psum | solution.py:42
  17.1 0.7 convert_element_type.65
  17.8 3.5 fusion.9
  21.4 150.1 %all-gather.3.cloned.1.call-done = bf16[1024,4096]{1,0:T(8,128)(2,1)} async-done(((bf16[256,4096]{1,0:T(8,128)(2,1)}), bf16[1024,4096]{1,0:T(8,128)(2,1)}) %all-gather.3.cloned.1.call-update) | async-done | bytes 8388624 | tf_op jit(solution)/shard_map/all_gather | solution.py:47
  171.5 5.7 convolution_convert_fusion.2
  177.3 1.0 copy.8
  178.3 7.1 %convolution_convert_fusion.3 = bf16[1024,256]{0,1:T(8,128)(2,1)} fusion(bf16[1024,4096]{1,0:T(8,128)(2,1)} %all-gather.3.cloned.1.call-done, bf16[4096,256]{1,0:T(8,128)(2,1)} %param.11), kind=kOutput, calls=%fused_computation.23 | convolution fusion | flops 2147745792 | bytes 11010048 | tf_op jit(solution)/shard_map/dot_general | solution.py:52
  185.4 0.6 reduce-scatter.3.cloned.1.call-start
  186.0 42.6 %convolution_convert_fusion.1 = bf16[1024,4096]{1,0:T(8,128)(2,1)} fusion(bf16[1024,4096]{1,0:T(8,128)(2,1)} %all-gather.3.cloned.1.call-done, bf16[4096,4096]{1,0:T(8,128)(2,1)} %param.9), kind=kOutput, calls=%fused_computation.9 | convolution fusion | flops 34363932672 | bytes 50331648 | tf_op jit(solution)/shard_map/dot_general | solution.py:50
  230.0 1.0 fusion.12
  230.9 1.9 multiply_cosine_fusion
  232.8 1.1 reshape_squeeze_stack.8
  234.4 64.3 %reduce-scatter.3.cloned.1.call-done = bf16[256,4096]{1,0:T(8,128)(2,1)} async-done(((bf16[1024,4096]{1,0:T(8,128)(2,1)}), bf16[256,4096]{1,0:T(8,128)(2,1)}) %reduce-scatter.3.cloned.1.call-update) | async-done | bytes 2097168 | tf_op jit(solution)/shard_map/reduce_scatter | solution.py:61
  298.7 2.1 convert_bitcast_fusion
  300.8 0.8 copy.15
  301.5 1.6 multiply_subtract_fusion
  303.2 4.4 copy.9
  307.5 4.5 copy.10
  312.0 18.3 %fusion.21 = (f32[2,16,256]{2,1,0:T(8,128)S(1)}, f32[2,16,256,1024]{2,3,1,0:T(8,128)}) fusion(pred[256,1024]{0,1:T(8,128)(4,1)S(1)} %copy-done.2, bf16[1024,2,64]{2,0,1:T(8,128)(2,1)S(1)} %get-tuple-element.26, bf16[1024,2,64]{2,0,1:T(8,128)(2,1)S(1)} %get-tuple-element.25, f32[256,2,16,64]{3,0,2,1:T(8,128)} %bitcast.50, f32[256,2,16,64]{3,0,2,1:T(8,128)} %bitcast.49), kind=kOutput, calls=%fused_computation.43 | convolution fusion | flops 2176844800 | bytes 38567936 | tf_op jit(solution)/shard_map/while/body/eval_jaxpr/sub | solution.py:103
  330.3 13.2 %fusion.11 = bf16[2,128,16,256]{3,1,2,0:T(8,128)(2,1)} fusion(f32[2,16,256,1024]{2,3,1,0:T(8,128)} %get-tuple-element.43, f32[2,16,256]{2,1,0:T(8,128)S(1)} %get-tuple-element.42, bf16[1024,2,128]{0,2,1:T(8,128)(2,1)S(1)} %copy-done.4), kind=kOutput, calls=%fused_computation.21 | convolution fusion | flops 2165309440 | bytes 36208640 | tf_op jit(solution)/shard_map/while/body/eval_jaxpr/cpts,scd->tcpd/dot_general | solution.py:106
  343.6 59.5 %all-gather.5.cloned.1.call-done = bf16[1024,4096]{0,1:T(8,128)(2,1)} async-done(((bf16[256,4096]{0,1:T(8,128)(2,1)}), bf16[1024,4096]{0,1:T(8,128)(2,1)}) %all-gather.5.cloned.1.call-update) | async-done | bytes 8388624 | tf_op jit(solution)/shard_map/all_gather | solution.py:112
  403.1 43.4 %convolution_convert_fusion = bf16[1024,4096]{1,0:T(8,128)(2,1)} fusion(bf16[1024,4096]{0,1:T(8,128)(2,1)} %all-gather.5.cloned.1.call-done, bf16[4096,4096]{1,0:T(8,128)(2,1)} %param.12), kind=kOutput, calls=%fused_computation.8 | convolution fusion | flops 34363932672 | bytes 50331648 | tf_op jit(solution)/shard_map/dot_general | solution.py:111
  446.5 144.6 %reduce-scatter.5.cloned.1.call-done = bf16[256,4096]{1,0:T(8,128)(2,1)} async-done(((bf16[1024,4096]{1,0:T(8,128)(2,1)}), bf16[256,4096]{1,0:T(8,128)(2,1)}) %reduce-scatter.5.cloned.1.call-update) | async-done | bytes 2097168 | tf_op jit(solution)/shard_map/reduce_scatter | solution.py:116
  (27 shorter events, 1.9 us)
Async XLA Ops:
  6.5 165.0 %copy-start = (bf16[4096,256]{1,0:T(8,128)(2,1)S(1)}, bf16[4096,256]{1,0:T(8,128)(2,1)}, u32[]{:S(2)}) copy-start(bf16[4096,256]{1,0:T(8,128)(2,1)} %param.10) | copy-start | bytes 6291460
  6.5 165.0 %all-gather.3.cloned.1.call-start = ((), (), s32[]{:S(2)}) async-start(), calls=%async_computation.2 | async-start | bytes 10485760 | tf_op jit(solution)/shard_map/all_gather | solution.py:47
  21.4 211.4 %all-reduce.3.cloned.1.call-start = ((), (), s32[]{:S(2)}) async-start(), calls=%async_computation.6 | async-start | bytes 2097152 | tf_op jit(solution)/shard_map/psum | solution.py:65
  185.4 113.3 %reduce-scatter.3.cloned.1.call-start = ((), (), s32[]{:S(2)}) async-start(), calls=%async_computation.3 | async-start | bytes 10485760 | tf_op jit(solution)/shard_map/reduce_scatter | solution.py:61
  228.6 0.7 copy-start.3
  228.7 174.4 %all-gather.5.cloned.1.call-start = ((), (), s32[]{:S(2)}) async-start(), calls=%async_computation.4 | async-start | bytes 10485760 | tf_op jit(solution)/shard_map/all_gather | solution.py:112
  307.5 4.5 copy-start.2
  312.0 18.3 %copy-start.4 = (bf16[1024,2,128]{0,2,1:T(8,128)(2,1)S(1)}, bf16[1024,2,128]{0,2,1:T(8,128)(2,1)}, u32[]{:S(2)}) copy-start(bf16[1024,2,128]{0,2,1:T(8,128)(2,1)} %get-tuple-element.22) | copy-start | bytes 1572868
  343.5 247.6 %reduce-scatter.5.cloned.1.call-start = ((), (), s32[]{:S(2)}) async-start(), calls=%async_computation.5 | async-start | bytes 10485760 | tf_op jit(solution)/shard_map/reduce_scatter | solution.py:116
  446.5 144.7 %copy-start.1 = (bf16[4096,256]{1,0:T(8,128)(2,1)S(1)}, bf16[4096,256]{1,0:T(8,128)(2,1)}, u32[]{:S(2)}) copy-start(bf16[4096,256]{1,0:T(8,128)(2,1)} %param.10) | copy-start | bytes 6291460
Sparse Core Ops, SparseCore 0:
  21.5 149.9 all-gather.2
  185.5 34.4 all-reduce.2
  228.8 69.8 reduce-scatter.2
  343.7 59.3 all-gather.4
  446.6 144.4 reduce-scatter.4
where the time goes:
time: 603 us; the launch traced here: 598 us
  waiting for transfers between devices  419 us (69%)
  matrix products  130 us (22%)
  other arithmetic  15.1 us (3%)
  between operations  13.5 us (2%)
  local copies, waits for them, and re-layouts  11.2 us (2%)
  blocking collectives  8.34 us (1%)
    all_gather x1, waiting for transfers between devices, body(): piece = lax.all_gather(normed, 'ffn', axis=0, tiled=True)  150 us
    reduce_scatter x1, waiting for transfers between devices, body(): lax.psum_scatter(terms.astype(jnp.bfloat16), 'ffn', scatter_dimension=0,...  145 us
    reduce_scatter x1, waiting for transfers between devices, body(): lax.psum_scatter(query_part.astype(jnp.bfloat16), ('wid', 'sub'), scatter...  64.3 us
    all_gather x1, waiting for transfers between devices, body(): lax.all_gather(attended, ('wid', 'sub'), axis=0, tiled=True)  59.5 us
    dot_general x1, matrix products, body(): jnp.dot(lax.all_gather(attended, ('wid', 'sub'), axis=0, tiled=True), out...  43.4 us
    dot_general x1, matrix products, body(): jnp.dot(piece, query_weight, preferred_element_type=jnp.float32)  42.6 us
    sub x1, matrix products, attend(): weights = jnp.exp(masked - highest)  18.3 us
    dot_general x1, matrix products, attend(): jnp.einsum('cpts,scd->tcpd', probs, values, preferred_element_type=jnp.fl...  13.2 us
  transfers between devices with their start and end apart: 5, of which 4 were waited for; matrix products, arithmetic and copies ran while one was open for 8% of the time, Pallas kernels for 0%

commit v1 on v0

v1 whole, which is shorter than its diff:
```python
import jax
import jax.numpy as jnp
import numpy as np
from jax import lax
from jax.sharding import PartitionSpec as P

KVH = 8
HD = 128


EPS = 1e-05
THETA = 500000.0
NEGATIVE = -1e30
CHAINS = 2


def swapped(value, axis, distance):
    mask = 2**distance
    pairs = [(source, source ^ mask) for source in range(lax.axis_size(axis))]
    return lax.ppermute(value, axis, pairs)


def rope_tables(positions):
    half = HD // 2
    freqs = THETA ** (-(jnp.arange(half, dtype=jnp.float32) * 2.0 / HD))
    angles = positions.astype(jnp.float32)[:, None] * freqs[None, :]
    return (jnp.cos(angles), jnp.sin(angles))


def rotate(tensor, cosine, sine):
    half = HD // 2
    first = tensor[..., :half]
    second = tensor[..., half:]
    cosine = cosine[:, None, :]
    sine = sine[:, None, :]
    return jnp.concatenate(
        [first * cosine - second * sine, second * cosine + first * sine], axis=-1
    )


def block_orders(count):
    return np.array(
        [sorted(range(count), key=lambda b: (abs(b - z), b)) for z in range(count)], dtype=np.int32
    )


def pick(choices, wanted, place):
    used = sorted({w for w in wanted if w is not None})
    result = choices[used[0]]
    for option in used[1:]:
        table = jnp.asarray(np.array([w == option for w in wanted]))
        result = jnp.where(table[place], choices[option], result)
    return result


def body(states, norm_gain, query_weight, key_weight, value_weight, output_weight, segments):
    n = lax.axis_size("ffn")
    place = lax.axis_index("ffn")
    inner = lax.axis_size(("wid", "sub"))
    inner_at = lax.axis_index(("wid", "sub"))
    orders = block_orders(n)
    slots = np.argsort(orders, axis=1)
    rows = states.shape[0]
    total_rows = rows * n
    query_cols = query_weight.shape[1]
    key_cols = key_weight.shape[1]

    from_below, from_above = {0: states}, {0: states}
    for s in range(1, n):
        from_below[s] = lax.ppermute(
            from_below[s - 1], "ffn", [(i, i + 1) for i in range(s - 1, n - 1)]
        )
        from_above[s] = lax.ppermute(
            from_above[s - 1], "ffn", [(i, i - 1) for i in range(1, n - s + 1)]
        )
    arrived = {}
    for s in range(n):
        arrived[s], arrived[-s] = from_above[s], from_below[s]

    wide_states = states.astype(jnp.float32)
    width = states.shape[1] * inner
    square_sum = lax.psum(jnp.sum(wide_states * wide_states, axis=1), ("wid", "sub"))
    own_scaling = lax.rsqrt(square_sum / width + EPS)
    all_scaling = lax.all_gather(own_scaling, "ffn", axis=0, tiled=False)
    gain = norm_gain.astype(jnp.float32)[None, :]

    order_here = jnp.asarray(orders)[place]
    query_rows = rows // inner
    slot_queries, slot_kv, slot_row_ids, slot_products = [], [], [], []
    heads_here = query_cols // HD
    for slot in range(n):
        block = order_here[slot]
        steps = [int(orders[z][slot]) - z for z in range(n)]
        choices = {step: arrived[step] for step in sorted(set(steps))}
        if slot > 0:
            choices, _ = lax.optimization_barrier((choices, query_part))
        piece = pick(choices, steps, place)
        scaling = lax.dynamic_index_in_dim(all_scaling, block, 0, keepdims=False)[:, None]
        normed = (piece.astype(jnp.float32) * scaling * gain).astype(jnp.bfloat16)
        kv_part = jnp.stack(
            [
                jnp.dot(normed, key_weight, preferred_element_type=jnp.float32).astype(jnp.bfloat16),
                jnp.dot(normed, value_weight, preferred_element_type=jnp.float32).astype(jnp.bfloat16),
            ]
        )
        if slot > 0:
            kv_part, slot_kv[-1] = lax.optimization_barrier((kv_part, slot_kv[-1]))
        slot_kv.append(lax.psum(kv_part, ("wid", "sub")))
        query_part = jnp.dot(normed, query_weight, preferred_element_type=jnp.float32).astype(
            jnp.bfloat16
        )
        slot_products.append(query_part)

    for slot in range(n):
        block = order_here[slot]
        query_sum = lax.psum_scatter(
            slot_products[slot], ("wid", "sub"), scatter_dimension=0, tiled=True
        ).astype(jnp.float32)
        row_ids = block * rows + inner_at * query_rows + jnp.arange(query_rows, dtype=jnp.int32)
        query_cos, query_sin = rope_tables(row_ids)
        queries = (
            rotate(query_sum.reshape(query_rows, heads_here, HD), query_cos, query_sin)
            * HD ** (-0.5)
        ).astype(jnp.bfloat16)
        slot_queries.append(queries)
        slot_row_ids.append(row_ids)

    stacked = jnp.stack(slot_kv)
    slot_of = jnp.asarray(slots.astype(np.int32))[place]
    kv_stack = jnp.concatenate(
        [lax.dynamic_index_in_dim(stacked, slot_of[b], 0, keepdims=False) for b in range(n)], axis=1
    )
    reach = max(1, n // KVH)
    for bit_number in range(reach.bit_length() - 1):
        partner = swapped(kv_stack, "ffn", bit_number)
        lower = place // 2**bit_number % 2 == 0
        kv_stack = jnp.where(
            lower,
            jnp.concatenate([kv_stack, partner], axis=2),
            jnp.concatenate([partner, kv_stack], axis=2),
        )
    kv_heads = kv_stack.shape[2] // HD
    per_group = heads_here // kv_heads
    all_rows = jnp.arange(total_rows, dtype=jnp.int32)
    cosine, sine = rope_tables(all_rows)
    keys = rotate(
        kv_stack[0].astype(jnp.float32).reshape(total_rows, kv_heads, HD), cosine, sine
    ).astype(jnp.bfloat16)
    values = kv_stack[1].reshape(total_rows, kv_heads, HD)

    def attend(queries, row_ids):
        queries = queries.reshape(query_rows, kv_heads, per_group, HD)
        query_segments = lax.dynamic_slice_in_dim(segments, row_ids[0], query_rows)
        allowed = (query_segments[:, None] == segments[None, :]) & (
            all_rows[None, :] <= row_ids[:, None]
        )
        scores = jnp.einsum("tcpd,scd->cpts", queries, keys, preferred_element_type=jnp.float32)
        masked = jnp.where(allowed[None, None], scores, NEGATIVE)
        highest = jnp.max(masked, axis=-1, keepdims=True)
        weights = jnp.exp(masked - highest)
        total = jnp.sum(weights, axis=-1, keepdims=True)
        probs = (weights / total).astype(jnp.bfloat16)
        result = jnp.einsum("cpts,scd->tcpd", probs, values, preferred_element_type=jnp.float32)
        return result.astype(jnp.bfloat16).reshape(query_rows, heads_here * HD)

    terms = [None] * n
    for slot in reversed(range(n)):
        attended = attend(slot_queries[slot], slot_row_ids[slot])
        terms[slot] = jnp.dot(
            lax.all_gather(attended, ("wid", "sub"), axis=0, tiled=True),
            output_weight,
            preferred_element_type=jnp.float32,
        ).astype(jnp.bfloat16)

    cols = output_weight.shape[1]
    outs = []
    for chain in range(CHAINS):
        part = [t[:, chain * cols // CHAINS : (chain + 1) * cols // CHAINS] for t in terms]
        below = above = None
        for r in range(n - 1, 0, -1):
            up_wanted = [int(slots[z][z + r]) if z + r < n else None for z in range(n)]
            down_wanted = [int(slots[z][z - r]) if z - r >= 0 else None for z in range(n)]
            up = pick(part, up_wanted, place)
            down = pick(part, down_wanted, place)
            if below is not None:
                up = (up.astype(jnp.float32) + below.astype(jnp.float32)).astype(jnp.bfloat16)
                down = (down.astype(jnp.float32) + above.astype(jnp.float32)).astype(jnp.bfloat16)
            below = lax.ppermute(up, "ffn", [(i, i + 1) for i in range(n - r)])
            above = lax.ppermute(down, "ffn", [(i, i - 1) for i in range(r, n)])
        total = part[0].astype(jnp.float32)
        if below is not None:
            total = total + below.astype(jnp.float32) + above.astype(jnp.float32)
        outs.append(total.astype(jnp.bfloat16))
    return jnp.concatenate(outs, axis=1)


def solution(mesh):
    in_specs = (
        P(("grp", "ffn"), ("wid", "sub")),
        P(("wid", "sub")),
        P(("wid", "sub"), "ffn"),
        P(("wid", "sub"), "ffn"),
        P(("wid", "sub"), "ffn"),
        P("ffn", ("wid", "sub")),
        P("grp"),
    )
    out_specs = P(("grp", "ffn"), ("wid", "sub"))
    return jax.shard_map(body, mesh=mesh, in_specs=in_specs, out_specs=out_specs, check_vma=False)
```

time: 603 us -> 617 us (1.023)
  waiting for transfers between devices: 419 us -> 212 us
  matrix products: 130 us -> 187 us
  starting transfers between devices: 0.87 us -> 53.5 us
  other arithmetic: 15.1 us -> 53 us
  blocking collectives: 8.34 us -> 42.9 us
  between operations: 13.5 us -> 32.6 us
  local copies, waits for them, and re-layouts: 11.2 us -> 26.2 us
    all_gather x1 -> x0, waiting for transfers between devices: 150 us -> none  [body(): piece = lax.all_gather(normed, 'ffn', axis=0, tiled=True)]
    reduce_scatter x2 -> x4, waiting for transfers between devices: 209 us -> 76.8 us  [body(): lax.psum_scatter(slot_products[slot], ('wid', 'sub'), scatter_dimension=0...]
    ppermute x0 -> x18, waiting for transfers between devices: none -> 121 us  [the longest x3 55.9 us: body(): lax.ppermute(from_above[s - 1], 'ffn', [(i, i - 1) for i in range(1, n -...]
    ppermute x0 -> x18, starting transfers between devices: none -> 52.2 us  [the longest x6 27.4 us: body(): below = lax.ppermute(up, 'ffn', [(i, i + 1) for i in range(n - r)])]
    all_gather x1 -> x4, waiting for transfers between devices: 59.5 us -> 8.09 us  [body(): lax.all_gather(attended, ('wid', 'sub'), axis=0, tiled=True)]
    all_gather x0 -> x1, blocking collectives: none -> 36.1 us  [body(): all_scaling = lax.all_gather(own_scaling, 'ffn', axis=0, tiled=False)]
    convert_element_type x2 -> x9, other arithmetic: 4.24 us -> 32.1 us  [the longest x3 13.9 us: body(): normed = (piece.astype(jnp.float32) * scaling * gain).astype(jnp.bfloat16)]
    dot_general x1 -> x4, matrix products: 43.4 us -> 64.1 us  [body(): jnp.dot(lax.all_gather(attended, ('wid', 'sub'), axis=0, tiled=True), out...]
  transfers between devices with their start and end apart: 5 -> 30, of which waited for: 4 -> 16; matrix products, arithmetic and copies ran while one was open for 8% -> 42% of each run, Pallas kernels for 0% -> 0%
where the time goes in v1:
time: 617 us; the launch traced here: 608 us
  waiting for transfers between devices  212 us (34%)
  matrix products  187 us (30%)
  starting transfers between devices  53.5 us (9%)
  other arithmetic  53 us (9%)
  blocking collectives  42.9 us (7%)
  between operations  32.6 us (5%)
  local copies, waits for them, and re-layouts  26.2 us (4%)
    reduce_scatter x4, waiting for transfers between devices, body(): lax.psum_scatter(slot_products[slot], ('wid', 'sub'), scatter_dimension=0...  76.8 us
    dot_general x4, matrix products, body(): jnp.dot(normed, query_weight, preferred_element_type=jnp.float32)  67 us
    dot_general x4, matrix products, body(): jnp.dot(lax.all_gather(attended, ('wid', 'sub'), axis=0, tiled=True), out...  64.1 us
    ppermute x3, waiting for transfers between devices, body(): lax.ppermute(from_above[s - 1], 'ffn', [(i, i - 1) for i in range(1, n -...  55.9 us
    ppermute x6, waiting for transfers between devices, body(): below = lax.ppermute(up, 'ffn', [(i, i + 1) for i in range(n - r)])  46.5 us
    all_gather x1, blocking collectives, body(): all_scaling = lax.all_gather(own_scaling, 'ffn', axis=0, tiled=False)  36.1 us
    sub x4, matrix products, attend(): weights = jnp.exp(masked - highest)  29.1 us
    ppermute x6, starting transfers between devices, body(): below = lax.ppermute(up, 'ffn', [(i, i + 1) for i in range(n - r)])  27.4 us
  transfers between devices with their start and end apart: 30, of which 16 were waited for; matrix products, arithmetic and copies ran while one was open for 42% of the time, Pallas kernels for 0%

profile of v1, /device:TPU:0, one launch (start us, length us, event | category | flops | bytes accessed | tf_op | source)
XLA Modules:
  0.0 607.6 jit_solution(3473505427959829928)
XLA Ops:
  30.2 36.1 %all-gather.1 = f32[4,1,256]{2,1,0:T(1,128)S(1)} all-gather(f32[1,1,256]{2,1,0:T(1,128)S(1)} %bitcast.230), channel_id=2, replica_groups=mesh['grp'=2,'ffn'=4,'wid'=2,'sub'=2] {'ffn'}, dimensions={0}, use_global_device_ids=true | all-gather | bytes 5120 | tf_op jit(solution)/shard_map/all_gather | solution.py:84
  75.9 16.8 %convolution_convert_fusion.7 = bf16[256,4096]{1,0:T(8,128)(2,1)} fusion(bf16[4096,4096]{1,0:T(8,128)(2,1)} %param.23, bf16[256,4096]{1,0:T(8,128)(2,1)} %param.21, f32[4096]{0:T(1024)S(1)} %convert_element_type.278, f32[256]{0:T(256)S(1)} %bitcast.246), kind=kOutput, calls=%fused_computation.29 | convolution fusion | flops 8595177472 | bytes 37766144 | tf_op jit(solution)/shard_map/dot_general | solution.py:109
  107.5 16.7 %convolution_convert_fusion.6 = bf16[256,4096]{1,0:T(8,128)(2,1)} fusion(bf16[256,4096]{1,0:T(8,128)(2,1)} %copy-done.5, bf16[4096,4096]{1,0:T(8,128)(2,1)} %param.23), kind=kOutput, calls=%fused_computation.28 | convolution fusion | flops 8590983168 | bytes 37748736 | tf_op jit(solution)/shard_map/dot_general | solution.py:109
  124.2 27.6 %collective-permute-done.3 = bf16[256,4096]{1,0:T(8,128)(2,1)} collective-permute-done((bf16[256,4096]{1,0:T(8,128)(2,1)}, bf16[256,4096]{1,0:T(8,128)(2,1)}, u32[]{:S(2)}, u32[]{:S(2)}) %collective-permute-start.3) | collective-permute-done | bytes 2097184 | tf_op jit(solution)/shard_map/ppermute | solution.py:73
  164.0 16.7 %convolution_convert_fusion.5 = bf16[256,4096]{1,0:T(8,128)(2,1)} fusion(bf16[256,4096]{1,0:T(8,128)(2,1)} %copy-done.3, bf16[4096,4096]{1,0:T(8,128)(2,1)} %param.23), kind=kOutput, calls=%fused_computation.27 | convolution fusion | flops 8590983168 | bytes 37748736 | tf_op jit(solution)/shard_map/dot_general | solution.py:109
  180.7 28.3 %collective-permute-done.5 = bf16[256,4096]{1,0:T(8,128)(2,1)} collective-permute-done((bf16[256,4096]{1,0:T(8,128)(2,1)}, bf16[256,4096]{1,0:T(8,128)(2,1)}, u32[]{:S(2)}, u32[]{:S(2)}) %collective-permute-start.5) | collective-permute-done | bytes 2097184 | tf_op jit(solution)/shard_map/ppermute | solution.py:73
  218.9 16.7 %convolution_convert_fusion.1 = bf16[256,4096]{1,0:T(8,128)(2,1)} fusion(bf16[256,4096]{1,0:T(8,128)(2,1)} %copy-done.6, bf16[4096,4096]{1,0:T(8,128)(2,1)} %param.23), kind=kOutput, calls=%fused_computation.23 | convolution fusion | flops 8590983168 | bytes 37748736 | tf_op jit(solution)/shard_map/dot_general | solution.py:109
  261.9 26.0 %reduce-scatter.11.cloned.1.call-done = bf16[64,4096]{1,0:T(8,128)(2,1)} async-done(((bf16[256,4096]{1,0:T(8,128)(2,1)}), bf16[64,4096]{1,0:T(8,128)(2,1)}) %reduce-scatter.11.cloned.1.call-update) | async-done | bytes 524304 | tf_op jit(solution)/shard_map/reduce_scatter | solution.py:116
  291.7 7.4 %fusion.72 = (f32[2,16,64]{2,1,0:T(8,128)S(1)}, f32[2,16,64,1024]{3,2,1,0:T(8,128)}) fusion(pred[64,1024]{1,0:T(8,128)(4,1)} %get-tuple-element.72, bf16[1024,2,128,1]{2,0,3,1:T(8,128)(2,1)} %maximum_bitcast_fusion, f32[64,2,16,64]{3,0,2,1:T(8,128)} %bitcast.220, f32[64,2,16,64]{3,0,2,1:T(8,128)S(1)} %bitcast.219), kind=kOutput, calls=%fused_computation.170 | convolution fusion | flops 543949824 | bytes 10035200 | tf_op jit(solution)/shard_map/sub | solution.py:160
  305.8 16.1 %reduce-scatter.7.cloned.1.call-done = bf16[64,4096]{1,0:T(8,128)(2,1)} async-done(((bf16[256,4096]{1,0:T(8,128)(2,1)}), bf16[64,4096]{1,0:T(8,128)(2,1)}) %reduce-scatter.7.cloned.1.call-update) | async-done | bytes 524304 | tf_op jit(solution)/shard_map/reduce_scatter | solution.py:116
  324.8 7.3 %fusion.73 = (f32[2,16,64]{2,1,0:T(8,128)S(1)}, f32[2,16,64,1024]{3,2,1,0:T(8,128)}) fusion(pred[64,1024]{1,0:T(8,128)(4,1)S(1)} %copy-done.15, bf16[1024,2,128,1]{2,0,3,1:T(8,128)(2,1)} %maximum_bitcast_fusion, f32[64,2,16,64]{3,0,2,1:T(8,128)S(1)} %bitcast.216, f32[64,2,16,64]{3,0,2,1:T(8,128)S(1)} %bitcast.213), kind=kOutput, calls=%fused_computation.171 | convolution fusion | flops 543949824 | bytes 10035200 | tf_op jit(solution)/shard_map/sub | solution.py:160
  338.5 17.4 %reduce-scatter.9.cloned.1.call-done = bf16[64,4096]{1,0:T(8,128)(2,1)} async-done(((bf16[256,4096]{1,0:T(8,128)(2,1)}), bf16[64,4096]{1,0:T(8,128)(2,1)}) %reduce-scatter.9.cloned.1.call-update) | async-done | bytes 524304 | tf_op jit(solution)/shard_map/reduce_scatter | solution.py:116
  358.8 7.2 %fusion.74 = (f32[2,16,64]{2,1,0:T(8,128)S(1)}, f32[2,16,64,1024]{3,2,1,0:T(8,128)}) fusion(pred[64,1024]{1,0:T(8,128)(4,1)S(1)} %get-tuple-element.71, bf16[1024,2,128,1]{2,0,3,1:T(8,128)(2,1)} %maximum_bitcast_fusion, f32[64,2,16,64]{3,0,2,1:T(8,128)S(1)} %bitcast.217, f32[64,2,16,64]{3,0,2,1:T(8,128)S(1)} %bitcast.214), kind=kOutput, calls=%fused_computation.172 | convolution fusion | flops 543949824 | bytes 10035200 | tf_op jit(solution)/shard_map/sub | solution.py:160
  372.7 17.4 %reduce-scatter.5.cloned.1.call-done = bf16[64,4096]{1,0:T(8,128)(2,1)} async-done(((bf16[256,4096]{1,0:T(8,128)(2,1)}), bf16[64,4096]{1,0:T(8,128)(2,1)}) %reduce-scatter.5.cloned.1.call-update) | async-done | bytes 524304 | tf_op jit(solution)/shard_map/reduce_scatter | solution.py:116
  393.0 7.2 %fusion.75 = (f32[2,16,64]{2,1,0:T(8,128)S(1)}, f32[2,16,64,1024]{3,2,1,0:T(8,128)}) fusion(pred[64,1024]{1,0:T(8,128)(4,1)S(1)} %get-tuple-element.69, bf16[1024,2,128,1]{2,0,3,1:T(8,128)(2,1)} %maximum_bitcast_fusion, f32[64,2,16,64]{3,0,2,1:T(8,128)S(1)} %bitcast.215, f32[64,2,16,64]{3,0,2,1:T(8,128)S(1)} %bitcast.212), kind=kOutput, calls=%fused_computation.173 | convolution fusion | flops 543949824 | bytes 10035200 | tf_op jit(solution)/shard_map/sub | solution.py:160
  406.2 8.0 %all-gather.13.cloned.1.call-done = bf16[256,4096]{1,0:T(8,128)(2,1)} async-done(((bf16[64,4096]{1,0:T(8,128)(2,1)}), bf16[256,4096]{1,0:T(8,128)(2,1)}) %all-gather.13.cloned.1.call-update) | async-done | bytes 2097168 | tf_op jit(solution)/shard_map/all_gather | solution.py:170
  414.3 16.4 %convolution_convert_fusion = bf16[256,4096]{1,0:T(8,128)(2,1)S(1)} fusion(bf16[256,4096]{1,0:T(8,128)(2,1)} %all-gather.13.cloned.1.call-done, bf16[4096,4096]{1,0:T(8,128)(2,1)} %param.26), kind=kOutput, calls=%fused_computation.22 | convolution fusion | flops 8590983168 | bytes 37748736 | tf_op jit(solution)/shard_map/dot_general | solution.py:169
  441.9 16.4 %convolution_convert_fusion.3 = bf16[256,4096]{1,0:T(8,128)(2,1)S(1)} fusion(bf16[256,4096]{1,0:T(8,128)(2,1)} %all-gather.9.cloned.1.call-done, bf16[4096,4096]{1,0:T(8,128)(2,1)} %param.26), kind=kOutput, calls=%fused_computation.25 | convolution fusion | flops 8590983168 | bytes 37748736 | tf_op jit(solution)/shard_map/dot_general | solution.py:169
  459.9 21.8 %collective-permute-done.6 = bf16[256,2048]{1,0:T(8,128)(2,1)} collective-permute-done((bf16[256,2048]{1,0:T(8,128)(2,1)}, bf16[256,2048]{1,0:T(8,128)(2,1)}, u32[]{:S(2)}, u32[]{:S(2)}) %collective-permute-start.6) | collective-permute-done | bytes 1048608 | tf_op jit(solution)/shard_map/ppermute | solution.py:188
  481.6 7.6 %add_convert_fusion.9 = (bf16[256,2048]{1,0:T(8,128)(2,1)S(1)}, bf16[256,2048]{1,0:T(8,128)(2,1)}, bf16[256,2048]{1,0:T(8,128)(2,1)}, bf16[256,2048]{1,0:T(8,128)(2,1)}) fusion(bf16[256,2048]{1,0:T(8,128)(2,1)} %collective-permute-done.6, pred[]{:T(512)} %bitcast.17, bf16[256,4096]{1,0:T(8,128)(2,1)S(1)} %convolution_convert_fusion.3, ...), kind=kLoop, calls=%fused_computation.58 | loop fusion | flops 10485760 | bytes 12582914 | tf_op jit(solution)/shard_map/convert_element_type | solution.py:186
  502.0 15.6 %convolution_convert_fusion.2 = bf16[256,4096]{1,0:T(8,128)(2,1)S(1)} fusion(bf16[256,4096]{1,0:T(8,128)(2,1)} %all-gather.11.cloned.1.call-done, bf16[4096,4096]{1,0:T(8,128)(2,1)} %param.26), kind=kOutput, calls=%fused_computation.24 | convolution fusion | flops 8590983168 | bytes 37748736 | tf_op jit(solution)/shard_map/dot_general | solution.py:169
  518.8 20.7 %collective-permute-done.7 = bf16[256,2048]{1,0:T(8,128)(2,1)} collective-permute-done((bf16[256,2048]{1,0:T(8,128)(2,1)S(1)}, bf16[256,2048]{1,0:T(8,128)(2,1)}, u32[]{:S(2)}, u32[]{:S(2)}) %collective-permute-start.7) | collective-permute-done | bytes 1048608 | tf_op jit(solution)/shard_map/ppermute | solution.py:188
  559.9 15.7 %convolution_convert_fusion.4 = bf16[256,4096]{1,0:T(8,128)(2,1)S(1)} fusion(bf16[256,4096]{1,0:T(8,128)(2,1)} %all-gather.7.cloned.1.call-done, bf16[4096,4096]{1,0:T(8,128)(2,1)} %param.26), kind=kOutput, calls=%fused_computation.26 | convolution fusion | flops 8590983168 | bytes 37748736 | tf_op jit(solution)/shard_map/dot_general | solution.py:169
  575.8 18.8 %collective-permute-done.17 = bf16[256,2048]{1,0:T(8,128)(2,1)} collective-permute-done((bf16[256,2048]{1,0:T(8,128)(2,1)}, bf16[256,2048]{1,0:T(8,128)(2,1)}, u32[]{:S(2)}, u32[]{:S(2)}) %collective-permute-start.17) | collective-permute-done | bytes 1048608 | tf_op jit(solution)/shard_map/ppermute | solution.py:189
  (201 shorter events, 169.2 us)
Async XLA Ops:
  6.5 97.0 %all-reduce.5.cloned.1.call-start = ((), (), s32[]{:S(2)}) async-start(), calls=%async_computation.4 | async-start | bytes 524288 | tf_op jit(solution)/shard_map/psum | solution.py:108
  6.5 86.1 %collective-permute-start.1 = (bf16[256,4096]{1,0:T(8,128)(2,1)}, bf16[256,4096]{1,0:T(8,128)(2,1)}, u32[]{:S(2)}, u32[]{:S(2)}) collective-permute-start(bf16[256,4096]{1,0:T(8,128)(2,1)} %param.21), channel_id=1, source_target_pairs={{4,0},{8,4},{12,8},{5,1},{9,5},{13,9},{6,2},{10,6},{14,10},{7,3},{... | collective-permute-start | bytes 6291464 | tf_op jit(solution)/shard_map/ppermute | solution.py:73
  8.0 84.7 %collective-permute-start = (bf16[256,4096]{1,0:T(8,128)(2,1)}, bf16[256,4096]{1,0:T(8,128)(2,1)}, u32[]{:S(2)}, u32[]{:S(2)}) collective-permute-start(bf16[256,4096]{1,0:T(8,128)(2,1)} %param.21), channel_id=1, source_target_pairs={{0,4},{4,8},{8,12},{1,5},{5,9},{9,13},{2,6},{6,10},{10,14},{3,7},{... | collective-permute-start | bytes 6291464 | tf_op jit(solution)/shard_map/ppermute | solution.py:70
  73.2 87.2 %all-reduce.7.cloned.1.call-start = ((), (), s32[]{:S(2)}) async-start(), calls=%async_computation.5 | async-start | bytes 524288 | tf_op jit(solution)/shard_map/psum | solution.py:108
  103.6 115.2 %all-reduce.9.cloned.1.call-start = ((), (), s32[]{:S(2)}) async-start(), calls=%async_computation.6 | async-start | bytes 524288 | tf_op jit(solution)/shard_map/psum | solution.py:108
  103.6 48.2 %collective-permute-start.3 = (bf16[256,4096]{1,0:T(8,128)(2,1)}, bf16[256,4096]{1,0:T(8,128)(2,1)}, u32[]{:S(2)}, u32[]{:S(2)}) collective-permute-start(bf16[256,4096]{1,0:T(8,128)(2,1)} %collective-permute-done.1), channel_id=1, source_target_pairs={{4,0},{8,4},{5,1},{9,5},{6,2},{10,6},{7,3},{11,7},{20,16},{24,20},... | collective-permute-start | bytes 6291464 | tf_op jit(solution)/shard_map/ppermute | solution.py:73
  104.9 46.9 %collective-permute-start.2 = (bf16[256,4096]{1,0:T(8,128)(2,1)}, bf16[256,4096]{1,0:T(8,128)(2,1)}, u32[]{:S(2)}, u32[]{:S(2)}) collective-permute-start(bf16[256,4096]{1,0:T(8,128)(2,1)} %collective-permute-done), channel_id=1, source_target_pairs={{4,8},{8,12},{5,9},{9,13},{6,10},{10,14},{7,11},{11,15},{20,24},{2... | collective-permute-start | bytes 6291464 | tf_op jit(solution)/shard_map/ppermute | solution.py:70
  160.5 93.5 %all-reduce.11.cloned.1.call-start = ((), (), s32[]{:S(2)}) async-start(), calls=%async_computation.7 | async-start | bytes 524288 | tf_op jit(solution)/shard_map/psum | solution.py:108
  160.5 48.5 %collective-permute-start.5 = (bf16[256,4096]{1,0:T(8,128)(2,1)}, bf16[256,4096]{1,0:T(8,128)(2,1)}, u32[]{:S(2)}, u32[]{:S(2)}) collective-permute-start(bf16[256,4096]{1,0:T(8,128)(2,1)} %collective-permute-done.3), channel_id=1, source_target_pairs={{4,0},{5,1},{6,2},{7,3},{20,16},{21,17},{22,18},{23,19}} | collective-permute-start | bytes 6291464 | tf_op jit(solution)/shard_map/ppermute | solution.py:73
  161.8 47.2 %collective-permute-start.4 = (bf16[256,4096]{1,0:T(8,128)(2,1)}, bf16[256,4096]{1,0:T(8,128)(2,1)}, u32[]{:S(2)}, u32[]{:S(2)}) collective-permute-start(bf16[256,4096]{1,0:T(8,128)(2,1)} %collective-permute-done.2), channel_id=1, source_target_pairs={{8,12},{9,13},{10,14},{11,15},{24,28},{25,29},{26,30},{27,31}} | collective-permute-start | bytes 6291464 | tf_op jit(solution)/shard_map/ppermute | solution.py:70
  218.8 69.1 %reduce-scatter.11.cloned.1.call-start = ((), (), s32[]{:S(2)}) async-start(), calls=%async_computation.14 | async-start | bytes 2621440 | tf_op jit(solution)/shard_map/reduce_scatter | solution.py:116
  235.6 86.3 %reduce-scatter.7.cloned.1.call-start = ((), (), s32[]{:S(2)}) async-start(), calls=%async_computation.10 | async-start | bytes 2621440 | tf_op jit(solution)/shard_map/reduce_scatter | solution.py:116
  236.2 119.7 %reduce-scatter.9.cloned.1.call-start = ((), (), s32[]{:S(2)}) async-start(), calls=%async_computation.12 | async-start | bytes 2621440 | tf_op jit(solution)/shard_map/reduce_scatter | solution.py:116
  237.0 153.1 %reduce-scatter.5.cloned.1.call-start = ((), (), s32[]{:S(2)}) async-start(), calls=%async_computation.8 | async-start | bytes 2621440 | tf_op jit(solution)/shard_map/reduce_scatter | solution.py:116
  237.7 176.5 %all-gather.13.cloned.1.call-start = ((), (), s32[]{:S(2)}) async-start(), calls=%async_computation.15 | async-start | bytes 2621440 | tf_op jit(solution)/shard_map/all_gather | solution.py:170
  305.3 136.6 %all-gather.9.cloned.1.call-start = ((), (), s32[]{:S(2)}) async-start(), calls=%async_computation.11 | async-start | bytes 2621440 | tf_op jit(solution)/shard_map/all_gather | solution.py:170
  338.5 163.5 %all-gather.11.cloned.1.call-start = ((), (), s32[]{:S(2)}) async-start(), calls=%async_computation.13 | async-start | bytes 2621440 | tf_op jit(solution)/shard_map/all_gather | solution.py:170
  372.5 187.4 %all-gather.7.cloned.1.call-start = ((), (), s32[]{:S(2)}) async-start(), calls=%async_computation.9 | async-start | bytes 2621440 | tf_op jit(solution)/shard_map/all_gather | solution.py:170
  437.7 43.9 %collective-permute-start.6 = (bf16[256,2048]{1,0:T(8,128)(2,1)}, bf16[256,2048]{1,0:T(8,128)(2,1)}, u32[]{:S(2)}, u32[]{:S(2)}) collective-permute-start(bf16[256,2048]{1,0:T(8,128)(2,1)} %get-tuple-element.49), channel_id=1, source_target_pairs={{0,4},{1,5},{2,6},{3,7},{16,20},{17,21},{18,22},{19,23}} | collective-permute-start | bytes 3145736 | tf_op jit(solution)/shard_map/ppermute | solution.py:188
  440.0 41.6 %collective-permute-start.9 = (bf16[256,2048]{1,0:T(8,128)(2,1)}, bf16[256,2048]{1,0:T(8,128)(2,1)}, u32[]{:S(2)}, u32[]{:S(2)}) collective-permute-start(bf16[256,2048]{1,0:T(8,128)(2,1)} %get-tuple-element.49), channel_id=1, source_target_pairs={{12,8},{13,9},{14,10},{15,11},{28,24},{29,25},{30,26},{31,27}} | collective-permute-start | bytes 3145736 | tf_op jit(solution)/shard_map/ppermute | solution.py:189
  497.5 42.1 %collective-permute-start.7 = (bf16[256,2048]{1,0:T(8,128)(2,1)S(1)}, bf16[256,2048]{1,0:T(8,128)(2,1)}, u32[]{:S(2)}, u32[]{:S(2)}) collective-permute-start(bf16[256,2048]{1,0:T(8,128)(2,1)S(1)} %get-tuple-element.37), channel_id=1, source_target_pairs={{0,4},{4,8},{1,5},{5,9},{2,6},{6,10},{3,7},{7,11},{16,20},{20,24},... | collective-permute-start | bytes 3145736 | tf_op jit(solution)/shard_map/ppermute | solution.py:188
  545.2 30.4 %collective-permute-start.11 = (bf16[256,2048]{1,0:T(8,128)(2,1)}, bf16[256,2048]{1,0:T(8,128)(2,1)}, u32[]{:S(2)}, u32[]{:S(2)}) collective-permute-start(bf16[256,2048]{1,0:T(8,128)(2,1)} %get-tuple-element.47), channel_id=1, source_target_pairs={{4,0},{8,4},{12,8},{5,1},{9,5},{13,9},{6,2},{10,6},{14,10},{7,3},{... | collective-permute-start | bytes 3145736 | tf_op jit(solution)/shard_map/ppermute | solution.py:189
  552.8 41.7 %collective-permute-start.17 = (bf16[256,2048]{1,0:T(8,128)(2,1)}, bf16[256,2048]{1,0:T(8,128)(2,1)}, u32[]{:S(2)}, u32[]{:S(2)}) collective-permute-start(bf16[256,2048]{1,0:T(8,128)(2,1)} %get-tuple-element.48), channel_id=1, source_target_pairs={{4,0},{8,4},{12,8},{5,1},{9,5},{13,9},{6,2},{10,6},{14,10},{7,3},{... | collective-permute-start | bytes 3145736 | tf_op jit(solution)/shard_map/ppermute | solution.py:189
  554.1 41.5 %collective-permute-start.8 = (bf16[256,2048]{1,0:T(8,128)(2,1)S(1)}, bf16[256,2048]{1,0:T(8,128)(2,1)}, u32[]{:S(2)}, u32[]{:S(2)}) collective-permute-start(bf16[256,2048]{1,0:T(8,128)(2,1)S(1)} %get-tuple-element.35), channel_id=1, source_target_pairs={{0,4},{4,8},{8,12},{1,5},{5,9},{9,13},{2,6},{6,10},{10,14},{3,7},{... | collective-permute-start | bytes 3145736 | tf_op jit(solution)/shard_map/ppermute | solution.py:188
  (32 other events, 424.1 us)
Sparse Core Ops, SparseCore 0:
  73.4 30.1 all-reduce.4
  106.0 31.9 all-reduce.6
  160.6 34.4 all-reduce.8
  219.0 35.0 all-reduce.10
  256.4 31.4 reduce-scatter.10
  290.4 31.4 reduce-scatter.6
  324.4 31.4 reduce-scatter.8
  358.6 31.4 reduce-scatter.4
  391.6 22.5 all-gather.12
  415.7 22.5 all-gather.8
  439.8 22.5 all-gather.10
  463.9 22.5 all-gather.6
